TPU v7x, 32 devices: a whole 2x2x4 slice. The times are simulated.
32 devices in a mesh: ctx: 4 (over z), chan: 8 (over y, x, core).
Axes of the slice: x: 2, y: 2, z: 4, core: 2. Of those that a mesh axis runs over, the one named last changes fastest.
Arguments:
- tokens: bfloat16 [8192, 4096], P(('ctx', 'chan')), may hold values from -6 to 6
- in_weight: bfloat16 [3, 4096, 4096], P(None, None, 'chan'), may hold values from -0.09375 to 0.09375
- short_weight: float32 [3, 3, 4096], P(None, None, 'chan'), may hold values from -3 to 3
- decay_rate: float32 [16, 4096], P(None, 'chan'), may hold values from 2.4414063e-05 to 0.0333333333
- residue: float32 [16, 4096], P(None, 'chan'), may hold values from -1.5 to 1.5
- skip_gain: float32 [4096], P('chan'), may hold values from -4 to 4
- out_weight: bfloat16 [4096, 4096], P('chan'), may hold values from -0.09375 to 0.09375
Outputs:
- block_out: bfloat16 [8192, 4096], P(('ctx', 'chan'))
All inputs are finite; a program needn't handle non-finite values.
Results may differ from a plain program's by a relative error of at most 0.02.
Values may be sent and summed in bfloat16 or wider, within the bound.
A program may use at most 192 MiB of HBM per device.

v0:
```python
import jax
import jax.numpy as jnp
from jax import lax
from jax.sharding import PartitionSpec as P

HIGH = lax.Precision.HIGHEST


def from_behind(array, axis, by):
    size = lax.axis_size(axis)
    pairs = [(i, i + by) for i in range(size) if 0 <= i + by < size]
    return lax.ppermute(array, axis, pairs)


def prefix(array, axis, combine, identity):
    size, mine = (lax.axis_size(axis), lax.axis_index(axis))
    everything = jax.tree.map(
        lambda part, kind: lax.all_gather(part.astype(kind), axis),
        array,
        (jnp.bfloat16, jnp.bfloat16),
    )
    start = jax.tree.map(
        lambda part, zero: jnp.broadcast_to(jnp.asarray(zero, part.dtype), part.shape),
        array,
        identity,
    )

    def lap(k, before):
        reached = k < mine
        new = combine(
            before, jax.tree.map(lambda part, own: part[k].astype(own.dtype), everything, array)
        )
        return jax.tree.map(lambda a, b: jnp.where(reached, a, b), new, before)

    return lax.fori_loop(0, size, lap, start)


def merge_states(earlier, latter):
    return (earlier[0] * latter[0], latter[0] * earlier[1] + latter[1])


def local(tokens, in_weight, short_weight, decay_rate, residue, skip_gain, out_weight):
    group_chans = in_weight.shape[2]
    filter_taps = short_weight.shape[0]
    projected = jnp.einsum(
        "ld,jdc->ljc",
        lax.all_gather(tokens, "chan", axis=0, tiled=True),
        in_weight,
        preferred_element_type=jnp.float32,
    ).astype(jnp.bfloat16)
    seq_rows = projected.shape[0]
    earlier_rows = from_behind(projected[seq_rows - (filter_taps - 1) :], "ctx", 1)
    padded = jnp.concatenate([earlier_rows, projected], 0)
    features = jnp.zeros((seq_rows, 3, group_chans), jnp.float32)
    for offset in range(filter_taps):
        features = features + short_weight[offset] * padded[
            filter_taps - 1 - offset : filter_taps - 1 - offset + seq_rows
        ].astype(jnp.float32)
    query_part = features[:, 0]
    driven = features[:, 1] * features[:, 2]
    mode_gain = residue * jnp.sqrt(2.0 * decay_rate)
    block_len = 128
    block_count = seq_rows // block_len
    lag_steps = jnp.arange(block_len, dtype=jnp.float32)
    decay_table = jnp.exp(-decay_rate[:, None, :] * lag_steps[None, :, None])
    lag_filter = jnp.sum(decay_table * mode_gain[:, None, :], 0)
    row_idx = jnp.arange(block_len)[:, None]
    col_idx = jnp.arange(block_len)[None, :]
    lag_index = jnp.maximum(row_idx - col_idx, 0)
    toeplitz = jnp.where(
        (row_idx >= col_idx)[:, :, None], jnp.take(lag_filter, lag_index, axis=0), 0.0
    )
    blocked = driven.reshape(block_count, block_len, group_chans)
    inner_part = jnp.einsum("ijc,bjc->bic", toeplitz, blocked, precision=HIGH)
    block_ends = jnp.einsum("rjc,bjc->brc", decay_table[:, ::-1, :], blocked, precision=HIGH)
    block_pos = jnp.arange(block_count, dtype=jnp.float32)
    block_gap = block_pos[:, None] - 1.0 - block_pos[None, :]
    block_mix = jnp.where(
        (block_gap >= 0.0)[:, :, None, None],
        jnp.exp(
            -decay_rate[None, None] * block_len * jnp.maximum(block_gap, 0.0)[:, :, None, None]
        ),
        0.0,
    )
    before = jnp.einsum("xyrc,yrc->xrc", block_mix, block_ends, precision=HIGH)
    tail_weight = jnp.exp(
        -decay_rate[None] * block_len * (block_count - 1.0 - block_pos)[:, None, None]
    )
    own_state = jnp.sum(tail_weight * block_ends, 0)
    device_span = jnp.exp(-decay_rate * seq_rows)
    identity = (jnp.ones_like(device_span), jnp.zeros_like(own_state))
    entering = prefix((device_span, own_state), "ctx", merge_states, identity)[1]
    before = (
        before + jnp.exp(-decay_rate[None] * block_len * block_pos[:, None, None]) * entering[None]
    )
    rise_table = mode_gain[:, None, :] * decay_table * jnp.exp(-decay_rate)[:, None, :]
    carried = jnp.einsum("ric,brc->bic", rise_table, before, precision=HIGH)
    long_conv = (inner_part + carried).reshape(seq_rows, group_chans)
    gated = (query_part * (long_conv + skip_gain * driven)).astype(jnp.bfloat16)
    rounded = jnp.dot(gated, out_weight, preferred_element_type=jnp.float32).astype(jnp.bfloat16)
    return lax.psum_scatter(
        lax.optimization_barrier(rounded).astype(jnp.float32).astype(jnp.bfloat16),
        "chan",
        scatter_dimension=0,
        tiled=True,
    )


def solution(mesh):
    return jax.shard_map(
        local,
        mesh=mesh,
        in_specs=(
            P(("ctx", "chan"), None),
            P(None, None, "chan"),
            P(None, None, "chan"),
            P(None, "chan"),
            P(None, "chan"),
            P("chan"),
            P("chan", None),
        ),
        out_specs=P(("ctx", "chan"), None),
        check_vma=False,
    )
```

profile of v0, /device:TPU:0, one launch (start us, length us, event | category | flops | bytes accessed | tf_op | source)
XLA Modules:
  0.0 530.8 jit_solution(17703982446718400169)
XLA Ops:
  12.3 6.9 %multiply_reduce_fusion.1 = (f32[128,512]{0,1:T(8,128)S(1)}, f32[16,128,512]{1,0,2:T(8,128)}) fusion(f32[16,512]{0,1:T(8,128)S(1)} %copy.60, f32[16,512]{0,1:T(8,128)S(1)} %copy.59), kind=kLoop, calls=%fused_computation.39 | loop fusion | flops 3080192 | bytes 4521984 | tf_op jit(solution)/shard_map/reduce_sum | solution.py:66
  19.2 82.6 %all-gather.4.cloned.1.call-done = bf16[2048,4096]{1,0:T(8,128)(2,1)} async-done(((bf16[256,4096]{1,0:T(8,128)(2,1)}), bf16[2048,4096]{1,0:T(8,128)(2,1)}) %all-gather.4.cloned.1.call-update) | async-done | bytes 16777232 | tf_op jit(solution)/shard_map/all_gather | solution.py:47
  101.8 32.5 %fusion.11 = bf16[2048,3,512]{2,0,1:T(8,128)(2,1)S(1)} fusion(bf16[3,4096,512]{2,1,0:T(8,128)(2,1)} %param.10, bf16[2048,4096]{1,0:T(8,128)(2,1)} %all-gather.4.cloned.1.call-done), kind=kOutput, calls=%fused_computation.20 | convolution fusion | flops 25772949504 | bytes 35651584 | tf_op jit(solution)/shard_map/ld,jdc->ljc/dot_general | solution.py:45
  134.3 2.7 copy-done.2
  137.0 3.4 collective-permute-start
  140.4 13.4 %all-gather = bf16[64,512]{1,0:T(8,128)(2,1)S(1)} all-gather(bf16[16,512]{1,0:T(8,128)(2,1)S(1)} %get-tuple-element.137), channel_id=2, replica_groups=mesh['ctx'=4,'chan'=8] {'ctx'}, dimensions={0}, use_global_device_ids=true | all-gather | bytes 81920 | tf_op jit(solution)/shard_map/all_gather | solution.py:18
  153.8 7.2 %rev.3 = f32[16,128,512]{1,0,2:T(8,128)} reverse(f32[16,128,512]{1,0,2:T(8,128)} %get-tuple-element.134), dimensions={1} | reverse | bytes 8388608 | tf_op jit(solution)/shard_map/rev | solution.py:75
  161.4 64.4 %gather_fusion = f32[16384,512]{1,0:T(8,128)} fusion(f32[128,512]{1,0:T(8,128)S(1)} %copy.61, s32[16384]{0:T(1024)S(1)} %bitcast_clamp_fusion), kind=kCustom, calls=%fused_computation | custom fusion | bytes 67174400 | tf_op jit(solution)/shard_map/jit(_take)/gather | solution.py:71
  225.9 35.5 %copy.62 = f32[128,128,512]{1,0,2:T(8,128)} copy(f32[128,128,512]{2,1,0:T(8,128)} %bitcast.62) | data formatting | bytes 67108864 | tf_op jit(solution)/shard_map/jit(_take)/gather | solution.py:71
  261.4 10.9 %multiply_add_fusion = f32[2048,3,512]{2,0,1:T(8,128)S(1)} fusion(bf16[2048,3,512]{2,0,1:T(8,128)(2,1)} %copy-done.2, bf16[2,3,512]{2,0,1:T(2,128)(2,1)S(1)} %collective-permute-done, f32[3,512]{1,0:T(4,128)S(1)} %copy-done.10, f32[3,512]{1,0:T(4,128)S(1)} %copy-done.11, f32[3,512]{1,0:T(4,128)S(1)} %copy-done.9), kind=kLoop, calls=%fused_computation.14 | loop fusion | flops 44040192 | bytes 18898944 | tf_op jit(solution)/shard_map/add | solution.py:56
  272.3 3.8 slice_multiply_fusion
  276.0 1.9 copy-done
  278.0 5.5 %copy.63 = f32[16,128,512]{1,0,2:T(8,128)} copy(f32[16,128,512]{2,1,0:T(8,128)} %bitcast.63) | data formatting | bytes 8388608 | tf_op jit(solution)/shard_map/mul | solution.py:60
  283.4 12.6 %fusion.18 = (bf16[16,512]{0,1:T(8,128)(2,1)S(1)}, f32[512,16,16]{2,1,0:T(8,128)}) fusion(f32[16]{0:T(128)S(1)} %copy-done.15, f32[16,512]{0,1:T(8,128)S(1)} %copy.65, f32[16,128,512]{1,0,2:T(8,128)} %copy.63, f32[16,128,512]{1,0,2:T(8,128)} %rev.3), kind=kOutput, calls=%fused_computation.30 | convolution fusion | flops 201711616 | bytes 8962112 | tf_op jit(solution)/shard_map/rjc,bjc->brc/dot_general | solution.py:75
  296.1 3.0 copy.78
  299.2 2.1 multiply_reduce_fusion
  301.3 3.7 copy.77
  305.1 13.1 %all-gather.1 = bf16[64,512]{1,0:T(8,128)(2,1)S(1)} all-gather(bf16[16,512]{1,0:T(8,128)(2,1)S(1)} %copy.66), channel_id=3, replica_groups=mesh['ctx'=4,'chan'=8] {'ctx'}, dimensions={0}, use_global_device_ids=true | all-gather | bytes 81920 | tf_op jit(solution)/shard_map/all_gather | solution.py:18
  318.6 9.2 %fusion.17 = f32[512,16,128]{2,1,0:T(8,128)S(1)} fusion(f32[16,512,16]{0,2,1:T(8,128)} %copy.77, f32[16,512]{0,1:T(8,128)S(1)} %copy.68, f32[16,512]{0,1:T(8,128)S(1)} %copy.67, f32[16,512]{0,1:T(8,128)S(1)} %copy.65, f32[16,512]{0,1:T(8,128)S(1)} %copy-done.6, f32[16,512]{0,1:T(8,128)S(1)} %copy-done.4), kind=kOutput, calls=%fused_computation.28 | convolution fusion | flops 204865536 | bytes 4882432 | tf_op jit(solution)/shard_map/ric,brc->bic/dot_general | solution.py:97
  327.8 56.7 %add_bitcast_fusion = f32[16,128,512]{1,0,2:T(8,128)} fusion(f32[512,16,128]{2,1,0:T(8,128)S(1)} %fusion.17, f32[16,128,512]{1,0,2:T(8,128)S(1)} %copy-done.1, f32[128,128,512]{1,0,2:T(8,128)} %copy.62, pred[128,128]{1,0:T(8,128)(4,1)S(1)} %copy-done.7, pred[128,128]{1,0:T(8,128)(4,1)S(1)} %copy-done.8), kind=kOutput, calls=%fused_computation.31 | convolution fusion | flops 1628438528 | bytes 46170112 | tf_op jit(solution)/shard_map/ijc,bjc->bic/dot_general | solution.py:74
  384.5 5.3 %copy.69 = f32[16,128,512]{2,1,0:T(8,128)} copy(f32[16,128,512]{1,0,2:T(8,128)} %add_bitcast_fusion) | data formatting | bytes 8388608 | tf_op jit(solution)/shard_map/add | solution.py:98
  389.8 8.1 %fusion.15 = bf16[2048,512]{1,0:T(8,128)(2,1)S(1)} fusion(f32[2048,3,512]{2,0,1:T(8,128)} %copy-done, f32[16,128,512]{2,1,0:T(8,128)} %copy.69, f32[512]{0:T(512)S(1)} %copy-done.13), kind=kLoop, calls=%fused_computation.24 | loop fusion | flops 5242880 | bytes 18876416 | tf_op jit(solution)/shard_map/convert_element_type | solution.py:99
  397.9 11.7 %convolution_convert_fusion = bf16[2048,4096]{1,0:T(8,128)(2,1)} fusion(bf16[2048,512]{1,0:T(8,128)(2,1)S(1)} %fusion.15, bf16[512,4096]{1,0:T(8,128)(2,1)S(1)} %copy-done.16), kind=kOutput, calls=%fused_computation.13 | convolution fusion | flops 8598323200 | bytes 23068672 | tf_op jit(solution)/shard_map/dot_general | solution.py:100
  409.6 114.3 %reduce-scatter.2.cloned.1.call-done = bf16[256,4096]{1,0:T(8,128)(2,1)} async-done(((bf16[2048,4096]{1,0:T(8,128)(2,1)}), bf16[256,4096]{1,0:T(8,128)(2,1)}) %reduce-scatter.2.cloned.1.call-update) | async-done | bytes 2097168 | tf_op jit(solution)/shard_map/reduce_scatter | solution.py:101
  (59 shorter events, 6.6 us)
Async XLA Ops:
  6.5 95.3 %all-gather.4.cloned.1.call-start = ((), (), s32[]{:S(2)}) async-start(), calls=%async_computation.1 | async-start | bytes 18874368 | tf_op jit(solution)/shard_map/all_gather | solution.py:47
  7.3 516.7 %reduce-scatter.2.cloned.1.call-start = ((), (), s32[]{:S(2)}) async-start(), calls=%async_computation.2 | async-start | bytes 18874368 | tf_op jit(solution)/shard_map/reduce_scatter | solution.py:101
  8.2 126.1 %copy-start.3 = (f32[16,512]{0,1:T(8,128)}, f32[16,512]{0,1:T(8,128)S(1)}, u32[]{:S(2)}) copy-start(f32[16,512]{0,1:T(8,128)S(1)} %copy.59) | copy-start | bytes 98308
  8.4 126.0 %copy-start.5 = (f32[16,512]{0,1:T(8,128)}, f32[16,512]{0,1:T(8,128)S(1)}, u32[]{:S(2)}) copy-start(f32[16,512]{0,1:T(8,128)S(1)} %copy.60) | copy-start | bytes 98308
  134.3 2.7 copy-start.2
  137.0 124.3 %collective-permute-start = (bf16[2,3,512]{2,0,1:T(2,128)(2,1)S(1)}, bf16[2,3,512]{2,0,1:T(2,128)(2,1)S(1)}, u32[]{:S(2)}, u32[]{:S(2)}) collective-permute-start(bf16[2,3,512]{2,0,1:T(2,128)(2,1)S(1)} %slice.38), channel_id=1, source_target_pairs={{0,8},{8,16},{16,24},{1,9},{9,17},{17,25},{2,10},{10,18},{18,26},{... | collective-permute-start | bytes 18440 | tf_op jit(solution)/shard_map/ppermute | solution.py:12
  225.8 35.5 %copy-start.9 = (f32[3,512]{1,0:T(4,128)S(1)}, f32[3,512]{1,0:T(4,128)}, u32[]{:S(2)}) copy-start(f32[3,512]{1,0:T(4,128)} %get-tuple-element.140) | copy-start | bytes 18436
  225.9 35.5 %copy-start.10 = (f32[3,512]{1,0:T(4,128)S(1)}, f32[3,512]{1,0:T(4,128)}, u32[]{:S(2)}) copy-start(f32[3,512]{1,0:T(4,128)} %get-tuple-element.141) | copy-start | bytes 18436
  225.9 35.5 %copy-start.11 = (f32[3,512]{1,0:T(4,128)S(1)}, f32[3,512]{1,0:T(4,128)}, u32[]{:S(2)}) copy-start(f32[3,512]{1,0:T(4,128)} %get-tuple-element.142) | copy-start | bytes 18436
  272.2 5.7 %copy-start = (f32[2048,3,512]{2,0,1:T(8,128)}, f32[2048,3,512]{2,0,1:T(8,128)S(1)}, u32[]{:S(2)}) copy-start(f32[2048,3,512]{2,0,1:T(8,128)S(1)} %multiply_add_fusion) | copy-start | bytes 37748740
  278.0 5.5 %copy-start.15 = (f32[16]{0:T(128)S(1)}, f32[16]{0:T(128)}, u32[]{:S(2)}) copy-start(f32[16]{0:T(128)} %iota_subtract_fusion.1) | copy-start | bytes 196
  296.1 3.0 copy-start.12
  296.1 3.0 copy-start.14
  299.1 19.4 %copy-start.4 = (f32[16,512]{0,1:T(8,128)S(1)}, f32[16,512]{0,1:T(8,128)}, u32[]{:S(2)}) copy-start(f32[16,512]{0,1:T(8,128)} %copy-done.3) | copy-start | bytes 98308
  299.1 19.4 %copy-start.6 = (f32[16,512]{0,1:T(8,128)S(1)}, f32[16,512]{0,1:T(8,128)}, u32[]{:S(2)}) copy-start(f32[16,512]{0,1:T(8,128)} %copy-done.5) | copy-start | bytes 98308
  318.5 9.2 %copy-start.1 = (f32[16,128,512]{1,0,2:T(8,128)S(1)}, f32[16,128,512]{1,0,2:T(8,128)}, u32[]{:S(2)}) copy-start(f32[16,128,512]{1,0,2:T(8,128)} %copy.63) | copy-start | bytes 12582916
  318.5 9.2 %copy-start.7 = (pred[128,128]{1,0:T(8,128)(4,1)S(1)}, pred[128,128]{1,0:T(8,128)(4,1)}, u32[]{:S(2)}) copy-start(pred[128,128]{1,0:T(8,128)(4,1)} %get-tuple-element.145) | copy-start | bytes 49156
  318.5 9.2 %copy-start.8 = (pred[128,128]{1,0:T(8,128)(4,1)S(1)}, pred[128,128]{1,0:T(8,128)(4,1)}, u32[]{:S(2)}) copy-start(pred[128,128]{1,0:T(8,128)(4,1)} %get-tuple-element.146) | copy-start | bytes 49156
  384.5 5.3 %copy-start.13 = (f32[512]{0:T(512)S(1)}, f32[512]{0:T(512)}, u32[]{:S(2)}) copy-start(f32[512]{0:T(512)} %param.14) | copy-start | bytes 6148
  389.8 8.1 %copy-start.16 = (bf16[512,4096]{1,0:T(8,128)(2,1)S(1)}, bf16[512,4096]{1,0:T(8,128)(2,1)}, u32[]{:S(2)}) copy-start(bf16[512,4096]{1,0:T(8,128)(2,1)} %param.15) | copy-start | bytes 12582916
Sparse Core Ops, SparseCore 0:
  9.2 92.5 all-gather.3
  409.8 114.1 reduce-scatter.1
where the time goes:
time: 532 us; the launch traced here: 531 us
  waiting for transfers between devices  198 us (37%)
  local copies, waits for them, and re-layouts  132 us (25%)
  matrix products  123 us (23%)
  other arithmetic  35.2 us (7%)
  blocking collectives  26.5 us (5%)
  between operations  13.7 us (3%)
    reduce_scatter x1, waiting for transfers between devices, local(): lax.psum_scatter(lax.optimization_barrier(rounded).astype(jnp.float32).as...  114 us
    gather x2, local copies, waits for them, and re-layouts, local(): jnp.take(lag_filter, lag_index, axis=0)  99.9 us
    all_gather x1, waiting for transfers between devices, local(): lax.all_gather(tokens, 'chan', axis=0, tiled=True)  82.6 us
    dot_general x1, matrix products, local(): inner_part = jnp.einsum('ijc,bjc->bic', toeplitz, blocked, precision=HIGH)  56.7 us
    dot_general x1, matrix products, local(): jnp.einsum('ld,jdc->ljc', lax.all_gather(tokens, 'chan', axis=0, tiled=Tr...  32.5 us
    all_gather x2, blocking collectives, prefix(): lax.all_gather(part.astype(kind), axis)  26.5 us
    dot_general x1, matrix products, local(): jnp.einsum('rjc,bjc->brc', decay_table[:, ::-1, :], blocked, precision=HIGH)  12.6 us
    dot_general x1, matrix products, local(): jnp.dot(gated, out_weight, preferred_element_type=jnp.float32)  11.7 us
  transfers between devices with their start and end apart: 3, of which 2 were waited for; matrix products, arithmetic and copies ran while one was open for 22% of the time, Pallas kernels for 0%

commit v1 on v0

--- a/solution.py
+++ b/solution.py
@@ -1,7 +1,415 @@
+import functools
+
 import jax
 import jax.numpy as jnp
 from jax import lax
+from jax.experimental import pallas as pl
+from jax.experimental.pallas import tpu as pltpu
 from jax.sharding import PartitionSpec as P
+
+MESH = pl.DeviceIdType.MESH
+F32, BF16 = jnp.float32, jnp.bfloat16
+LANES, SUBS, PAD = 128, 8, 8
+CHAN = 8
+UNROLL = 4
+
+
+def kernel(
+    ctxs, tokens, in_w, short_w, decay, residue, skip, out_w, out,
+    grid_buf, w_buf, wo_buf, feat, excl, block_end, state, gated, gated16,
+    halo_buf, load_sem, ag_send, ag_recv, halo_send, halo_recv, st_send, st_recv,
+    cp_send, cp_recv, link_send, link_recv, credit, out_sem,
+):
+    ctx, me = lax.axis_index("ctx"), lax.axis_index("chan")
+    core, xpos, ypos = me % 2, (me // 2) % 2, me // 4
+    to_core, to_x, to_y = 1 - 2 * core, 2 - 4 * xpos, 4 - 8 * ypos
+    cp, xp, yp = me + to_core, me + to_x, me + to_y
+    diag = me + to_x + to_y
+    rows, width = tokens.shape
+    half = rows // 2
+    tiles = in_w.shape[2] // LANES
+    modes = decay.shape[0]
+    seq_rows = rows * CHAN
+    step_rows = rows // SUBS
+    top, low = pl.ds(0, half), pl.ds(half, half)
+
+    def send(src, dst, send_sem, recv_sem, chan=None, to_ctx=None):
+        where = {"chan": chan} if to_ctx is None else {"ctx": to_ctx}
+        return pltpu.make_async_remote_copy(
+            src_ref=src, dst_ref=dst, send_sem=send_sem, recv_sem=recv_sem,
+            device_id=where, device_id_type=MESH,
+        )
+
+    barrier = pltpu.get_barrier_semaphore()
+    for partner in (cp, xp, yp):
+        pl.semaphore_signal(barrier, inc=1, device_id={"chan": partner}, device_id_type=MESH)
+    for off in range(1, ctxs):
+        pl.semaphore_signal(
+            barrier, inc=1, device_id={"ctx": (ctx + off) % ctxs}, device_id_type=MESH
+        )
+
+    loads = [pltpu.make_async_copy(tokens, grid_buf.at[me], load_sem.at[0])]
+    loads += [
+        pltpu.make_async_copy(in_w.at[j], w_buf.at[j], load_sem.at[1 + j]) for j in range(3)
+    ]
+    loads += [pltpu.make_async_copy(out_w, wo_buf, load_sem.at[4])]
+    for load in loads:
+        load.start()
+    pl.semaphore_wait(barrier, 3 + ctxs - 1)
+
+    def hop(i, block, part, to, src=None):
+        src = grid_buf.at[block, part] if src is None else src
+        return send(src, grid_buf.at[block, part], ag_send.at[i], ag_recv.at[i], chan=to)
+
+    whole = pl.ds(0, rows)
+    sent = [
+        hop(0, me, top, xp, tokens.at[top]),
+        hop(1, me, low, yp, tokens.at[low]),
+        hop(2, me, whole, cp, tokens),
+        hop(3, me, low, xp, tokens.at[low]),
+        hop(4, me, top, yp, tokens.at[top]),
+    ]
+    for copy in sent:
+        copy.start()
+
+    def forward(i, block, part, to):
+        copy = hop(i, block, part, to)
+        copy.start()
+        sent.append(copy)
+
+    def arrived(i, block, part):
+        hop(i, block, part, cp).wait_recv()
+
+    def project(block):
+        start = pl.multiple_of(PAD + block * rows, SUBS)
+
+        def kind(j, _):
+            made = jnp.dot(grid_buf[block], w_buf[j], preferred_element_type=F32)
+            made = made.astype(BF16).astype(F32)
+            for l in range(tiles):
+                feat[j * tiles + l, pl.ds(start, rows), :] = made[:, l * LANES:(l + 1) * LANES]
+            return 0
+
+        lax.fori_loop(0, 3, kind, 0)
+
+    for load in loads[:4]:
+        load.wait()
+    project(me)
+    arrived(2, cp, whole)
+    project(cp)
+    arrived(0, xp, top)
+    forward(5, xp, top, yp)
+    forward(7, xp, top, cp)
+    arrived(1, yp, low)
+    forward(6, yp, low, xp)
+    forward(8, yp, low, cp)
+    arrived(3, xp, low)
+    forward(9, xp, low, cp)
+    arrived(4, yp, top)
+    forward(10, yp, top, cp)
+    project(xp)
+    project(yp)
+    arrived(7, cp + to_x, top)
+    arrived(9, cp + to_x, low)
+    project(cp + to_x)
+    arrived(8, cp + to_y, low)
+    arrived(10, cp + to_y, top)
+    project(cp + to_y)
+    arrived(5, diag, top)
+    forward(11, diag, top, cp)
+    arrived(6, diag, low)
+    forward(12, diag, low, cp)
+    project(diag)
+    arrived(11, diag + to_core, top)
+    arrived(12, diag + to_core, low)
+    project(diag + to_core)
+
+    tail = pl.ds(PAD + seq_rows - PAD, PAD)
+    halo_buf[...] = feat[:, tail, :]
+    halo = send(
+        halo_buf, feat.at[:, pl.ds(0, PAD)], halo_send, halo_recv, to_ctx=(ctx + 1) % ctxs
+    )
+
+    @pl.when(ctx < ctxs - 1)
+    def _():
+        halo.start()
+
+    for copy in sent:
+        copy.wait_send()
+    for partner in (cp, xp, yp):
+        pl.semaphore_signal(credit, inc=1, device_id={"chan": partner}, device_id_type=MESH)
+
+    def lanes_of(l):
+        return pl.ds(pl.multiple_of(l * LANES, LANES), LANES)
+
+    sub = lax.broadcasted_iota(jnp.int32, (modes, SUBS, LANES), 1)
+    wide = (modes, SUBS, LANES)
+
+    def first_pass(block):
+        base = PAD + block * rows
+
+        def tile(l, _):
+            rate = jnp.broadcast_to(decay[:, :, lanes_of(l)], wide)
+            pole = jnp.exp(-rate)
+            taps = [
+                [jnp.broadcast_to(short_w[k, j:j + 1, lanes_of(l)], (SUBS, LANES)) for j in range(3)]
+                for k in range(3)
+            ]
+
+            def at(i):
+                return pl.ds(base + i, SUBS, step_rows)
+
+            def steps(it, carry):
+                s, last, before = carry
+                for u in range(UNROLL):
+                    i = it * UNROLL + u
+                    now = [feat[j * tiles + l, at(i), :] for j in range(3)]
+                    made = [
+                        taps[0][j] * now[j] + taps[1][j] * last[j] + taps[2][j] * before[j]
+                        for j in range(3)
+                    ]
+                    driven = made[1] * made[2]
+                    feat[l, at(i), :] = made[0]
+                    feat[tiles + l, at(i), :] = driven
+                    s = pole * s + driven[None]
+                    last, before = now, last
+                return s, last, before
+
+            s, _, _ = lax.fori_loop(
+                0, step_rows // UNROLL, steps,
+                (
+                    jnp.zeros(wide, F32),
+                    [feat[j * tiles + l, at(-1), :] for j in range(3)],
+                    [feat[j * tiles + l, at(-2), :] for j in range(3)],
+                ),
+            )
+            for shift in (1, 2, 4):
+                fade = jnp.exp(-rate * float(step_rows * shift))
+                s = s + jnp.where(sub >= shift, pltpu.roll(s, shift, 1) * fade, 0.0)
+            excl[block, l] = jnp.where(sub >= 1, pltpu.roll(s, 1, 1), 0.0)
+            block_end[block, l] = s[:, SUBS - 1:SUBS, :]
+            return 0
+
+        lax.fori_loop(0, tiles, tile, 0)
+
+    def backwards(i, _):
+        first_pass(CHAN - 1 - i)
+        return 0
+
+    lax.fori_loop(0, CHAN - 1, backwards, 0)
+
+    @pl.when(ctx == 0)
+    def _():
+        feat[:, 0:PAD, :] = jnp.zeros((3 * tiles, PAD, LANES), F32)
+
+    @pl.when(ctx > 0)
+    def _():
+        halo.wait_recv()
+
+    @pl.when(ctx < ctxs - 1)
+    def _():
+        halo.wait_send()
+
+    first_pass(0)
+
+    def own_state(l, _):
+        fade = jnp.exp(-decay[:, :, lanes_of(l)] * float(rows))
+        total = block_end[0, l]
+        for block in range(1, CHAN):
+            total = fade * total + block_end[block, l]
+        state[ctx, l] = total
+        return 0
+
+    lax.fori_loop(0, tiles, own_state, 0)
+    state_copies = []
+    for off in range(1, ctxs):
+        copy = send(
+            state.at[ctx], state.at[ctx], st_send.at[off], st_recv.at[off],
+            to_ctx=(ctx + off) % ctxs,
+        )
+        copy.start()
+        state_copies.append(copy)
+    for off in range(1, ctxs):
+        source = (ctx + ctxs - off) % ctxs
+        send(
+            state.at[source], state.at[source], st_send.at[off], st_recv.at[off], to_ctx=source
+        ).wait_recv()
+
+    def enter(l, _):
+        rate = decay[:, :, lanes_of(l)]
+        s = jnp.zeros((modes, 1, LANES), F32)
+        for off in range(1, ctxs):
+            source = (ctx + ctxs - off) % ctxs
+            known = jnp.where(ctx >= off, 1.0, 0.0).astype(F32)
+            s = s + known * jnp.exp(-rate * float(seq_rows * (off - 1))) * state[source, l]
+        fade = jnp.exp(-rate * float(rows))
+        inner = jnp.exp(-jnp.broadcast_to(rate, wide) * (sub * step_rows).astype(F32))
+        for block in range(CHAN):
+            excl[block, l] = excl[block, l] + inner * s
+            s = fade * s + block_end[block, l]
+        return 0
+
+    lax.fori_loop(0, tiles, enter, 0)
+
+    def gate(block):
+        base = PAD + block * rows
+
+        def tile(l, _):
+            rate = jnp.broadcast_to(decay[:, :, lanes_of(l)], wide)
+            pole = jnp.exp(-rate)
+            gain = jnp.broadcast_to(residue[:, :, lanes_of(l)], wide) * jnp.sqrt(2.0 * rate)
+            direct = jnp.broadcast_to(skip[:, lanes_of(l)], (SUBS, LANES))
+
+            def steps(it, s):
+                for u in range(UNROLL):
+                    i = it * UNROLL + u
+                    at = pl.ds(base + i, SUBS, step_rows)
+                    driven = feat[tiles + l, at, :]
+                    s = pole * s + driven[None]
+                    y = jnp.sum(gain * s, axis=0) + direct * driven
+                    gated[l, pl.ds(i, SUBS, step_rows), :] = feat[l, at, :] * y
+                return s
+
+            lax.fori_loop(0, step_rows // UNROLL, steps, excl[block, l])
+            return 0
+
+        lax.fori_loop(0, tiles, tile, 0)
+        for l in range(tiles):
+            gated16[:, l * LANES:(l + 1) * LANES] = gated[l].astype(BF16)
+
+    cut = 512
+
+    def over_width(body):
+        def one(t, _):
+            body(pl.ds(pl.multiple_of(t * cut, cut), cut))
+            return 0
+
+        lax.fori_loop(0, width // cut, one, 0)
+
+    def multiply(slot, add):
+        def body(cols):
+            made = jnp.dot(gated16[...], wo_buf[:, cols], preferred_element_type=F32).astype(BF16)
+            if add:
+                made = (grid_buf[slot, :, cols].astype(F32) + made.astype(F32)).astype(BF16)
+            grid_buf[slot, :, cols] = made
+
+        over_width(body)
+
+    loads[4].wait()
+    pl.semaphore_wait(credit, 3)
+
+    def link(i, src_slot, dst_slot, part, to):
+        return send(
+            grid_buf.at[src_slot, part], grid_buf.at[dst_slot, part],
+            link_send.at[i], link_recv.at[i], chan=to,
+        )
+
+    linked = []
+
+    def go(*what):
+        copy = link(*what)
+        copy.start()
+        linked.append(copy)
+
+    to_other = []
+    for i, mine in enumerate((diag, xp, yp, me)):
+        stage = 7 + i % 2
+        gate(mine + to_core)
+        if i >= 2:
+            to_other[i - 2].wait_send()
+        multiply(stage, False)
+        copy = send(
+            grid_buf.at[stage], grid_buf.at[i], cp_send.at[i], cp_recv.at[i], chan=cp
+        )
+        copy.start()
+        to_other.append(copy)
+        gate(mine)
+        copy.wait_recv()
+        multiply(i, True)
+        if i == 0:
+            go(0, 0, 4, top, xp)
+            go(1, 0, 4, low, yp)
+        if i == 1:
+            go(2, 1, 5, top, xp)
+        if i == 2:
+            go(3, 2, 6, low, yp)
+
+    def join(dst, part, *slots):
+        def body(cols):
+            total = grid_buf[slots[0], part, cols].astype(F32)
+            for slot in slots[1:]:
+                total = total + grid_buf[slot, part, cols].astype(F32)
+            grid_buf[dst, part, cols] = total.astype(BF16)
+
+        over_width(body)
+
+    link(1, 0, 4, low, yp).wait_recv()
+    join(1, low, 1, 4)
+    go(4, 1, 5, low, xp)
+    link(0, 0, 4, top, xp).wait_recv()
+    join(2, top, 2, 4)
+    go(5, 2, 6, top, yp)
+    for copy in to_other[2:]:
+        copy.wait_send()
+    results = []
+    for h, part, early, late in ((0, top, (2, 5), (5, 6)), (1, low, (3, 6), (4, 5))):
+        link(early[0], 0, early[1], part, xp).wait_recv()
+        link(late[0], 0, late[1], part, xp).wait_recv()
+        join(7, part, 3, 5, 6)
+        result = pltpu.make_async_copy(grid_buf.at[7, part], out.at[part], out_sem.at[h])
+        result.start()
+        results.append(result)
+    for copy in linked:
+        copy.wait_send()
+    for copy in state_copies:
+        copy.wait_send()
+    for result in results:
+        result.wait()
+
+
+def local(ctxs, tokens, in_weight, short_weight, decay_rate, residue, skip_gain, out_weight):
+    rows, width = tokens.shape
+    chans = in_weight.shape[2]
+    modes = decay_rate.shape[0]
+    tiles = chans // LANES
+    seq_rows = rows * CHAN
+    any_spec = pl.BlockSpec(memory_space=pl.ANY)
+    vmem = pl.BlockSpec(memory_space=pltpu.VMEM)
+    dma = pltpu.SemaphoreType.DMA
+    return pl.pallas_call(
+        functools.partial(kernel, ctxs),
+        out_shape=jax.ShapeDtypeStruct((rows, width), BF16),
+        in_specs=[any_spec, any_spec, vmem, vmem, vmem, vmem, any_spec],
+        out_specs=any_spec,
+        scratch_shapes=[
+            pltpu.VMEM((CHAN + 1, rows, width), BF16),
+            pltpu.VMEM(in_weight.shape, BF16),
+            pltpu.VMEM(out_weight.shape, BF16),
+            pltpu.VMEM((3 * tiles, PAD + seq_rows, LANES), F32),
+            pltpu.VMEM((CHAN, tiles, modes, SUBS, LANES), F32),
+            pltpu.VMEM((CHAN, tiles, modes, 1, LANES), F32),
+            pltpu.VMEM((ctxs, tiles, modes, 1, LANES), F32),
+            pltpu.VMEM((tiles, rows, LANES), F32),
+            pltpu.VMEM((rows, chans), BF16),
+            pltpu.VMEM((3 * tiles, PAD, LANES), F32),
+            dma((5,)), dma((13,)), dma((13,)), dma, dma, dma((ctxs,)), dma((ctxs,)),
+            dma((4,)), dma((4,)), dma((6,)), dma((6,)),
+            pltpu.SemaphoreType.REGULAR, dma((2,)),
+        ],
+        compiler_params=pltpu.CompilerParams(
+            collective_id=0, has_side_effects=True, vmem_limit_bytes=62 * 2**20
+        ),
+        cost_estimate=pl.CostEstimate(
+            flops=2 * seq_rows * width * 4 * chans,
+            bytes_accessed=2 * 4 * width * chans + 4 * rows * width,
+            transcendentals=0,
+        ),
+    )(
+        tokens, in_weight, short_weight,
+        decay_rate.reshape(modes, 1, chans), residue.reshape(modes, 1, chans),
+        skip_gain.reshape(1, chans), out_weight,
+    )
+
 
 HIGH = lax.Precision.HIGHEST
 
@@ -39,7 +447,7 @@
     return (earlier[0] * latter[0], latter[0] * earlier[1] + latter[1])
 
 
-def local(tokens, in_weight, short_weight, decay_rate, residue, skip_gain, out_weight):
+def general(tokens, in_weight, short_weight, decay_rate, residue, skip_gain, out_weight):
     group_chans = in_weight.shape[2]
     filter_taps = short_weight.shape[0]
     projected = jnp.einsum(
@@ -107,8 +515,9 @@
 
 
 def solution(mesh):
+    square = mesh.shape["chan"] == CHAN
     return jax.shard_map(
-        local,
+        functools.partial(local, mesh.shape["ctx"]) if square else general,
         mesh=mesh,
         in_specs=(
             P(("ctx", "chan"), None),

time: 532 us -> 197 us (0.37)
  waiting for transfers between devices: 198 us -> 0 us
  Pallas kernels: 0 us -> 191 us
  local copies, waits for them, and re-layouts: 132 us -> 5.9 us
  matrix products: 123 us -> 0 us
  other arithmetic: 35.2 us -> 0 us
  blocking collectives: 26.5 us -> 0 us
  between operations: 13.7 us -> 0.01 us
    pallas_call x0 -> x1, Pallas kernels: none -> 191 us  [local(): pl.pallas_call(functools.partial(kernel, ctxs), out_shape=jax.ShapeDtypeS...]
    dot_general x5 -> x0, matrix products: 123 us -> none  [the longest x1 56.7 us: local(): inner_part = jnp.einsum('ijc,bjc->bic', toeplitz, blocked, precision=HIGH)]
    reduce_scatter x1 -> x0, waiting for transfers between devices: 114 us -> none  [local(): lax.psum_scatter(lax.optimization_barrier(rounded).astype(jnp.float32).as...]
    gather x2 -> x0, local copies, waits for them, and re-layouts: 99.9 us -> none  [local(): jnp.take(lag_filter, lag_index, axis=0)]
    all_gather x1 -> x0, waiting for transfers between devices: 82.6 us -> none  [local(): lax.all_gather(tokens, 'chan', axis=0, tiled=True)]
    all_gather x2 -> x0, blocking collectives: 26.5 us -> none  [prefix(): lax.all_gather(part.astype(kind), axis)]
    add x1 -> x0, other arithmetic: 10.9 us -> none  [local(): features + short_weight[offset] * padded[filter_taps - 1 - offset:filter_...]
    convert_element_type x1 -> x0, other arithmetic: 8.11 us -> none  [local(): gated = (query_part * (long_conv + skip_gain * driven)).astype(jnp.bfloat16)]
  transfers between devices with their start and end apart: 3 -> 0, of which waited for: 2 -> 0; matrix products, arithmetic and copies ran while one was open for 22% -> 0% of each run, Pallas kernels for 0% -> 0%
where the time goes in v1:
time: 197 us; the launch traced here: 196 us
  Pallas kernels  191 us (97%)
  local copies, waits for them, and re-layouts  5.9 us (3%)
    pallas_call x1, Pallas kernels, local(): pl.pallas_call(functools.partial(kernel, ctxs), out_shape=jax.ShapeDtypeS...  191 us

profile of v1, /device:TPU:0, one launch (start us, length us, event | category | flops | bytes accessed | tf_op | source)
XLA Modules:
  0.0 196.5 jit_solution(16678710349961350731)
XLA Ops:
  0.0 1.4 reshape.9.decay
  1.4 1.4 reshape.10.residue
  2.8 190.5 %shard_map.73 = bf16[256,4096]{1,0:T(8,128)(2,1)} custom-call(bf16[256,4096]{1,0:T(8,128)(2,1)} %tokens.1, bf16[3,4096,512]{2,1,0:T(8,128)(2,1)} %in_w.1, f32[3,3,512]{2,1,0:T(4,128)} %short_w.1, f32[16,1,512]{2,1,0:T(1,128)} %reshape.9.decay, f32[16,1,512]{2,1,0:T(1,128)} %reshape.10.residue, f32[1,512]{1,0:T(1,128)} %bitcast.1, bf16[512,4096]{1,0:T(8,128)(2,1)} %out_w.1), custom_call_target="tpu_custom_call" | custom-call | flops 34359738368 | bytes 20971520 | tf_op jit(solution)/shard_map/pallas_call | solution.py:379
  193.3 3.1 %copy.9 = bf16[256,4096]{1,0:T(8,128)(2,1)} copy(bf16[256,4096]{1,0:T(8,128)(2,1)} %shard_map.73) | data formatting | bytes 4194304

commit v2 on v1

--- a/solution.py
+++ b/solution.py
@@ -15,9 +15,9 @@
 
 
 def kernel(
-    ctxs, tokens, in_w, short_w, decay, residue, skip, out_w, out,
+    ctxs, tokens, in_w, short_w, decay_in, residue_in, skip, out_w, out,
     grid_buf, w_buf, wo_buf, feat, excl, block_end, state, gated, gated16,
-    halo_buf, load_sem, ag_send, ag_recv, halo_send, halo_recv, st_send, st_recv,
+    head, edge, decay, residue, load_sem, ag_send, ag_recv, halo_send, halo_recv, st_send, st_recv,
     cp_send, cp_recv, link_send, link_recv, credit, out_sem,
 ):
     ctx, me = lax.axis_index("ctx"), lax.axis_index("chan")
@@ -28,7 +28,7 @@
     rows, width = tokens.shape
     half = rows // 2
     tiles = in_w.shape[2] // LANES
-    modes = decay.shape[0]
+    modes = decay_in.shape[0]
     seq_rows = rows * CHAN
     step_rows = rows // SUBS
     top, low = pl.ds(0, half), pl.ds(half, half)
@@ -91,12 +91,108 @@
             return 0
 
         lax.fori_loop(0, 3, kind, 0)
-
+        head[block] = feat[:, pl.ds(start, PAD), :]
+        edge[block + 1] = feat[:, pl.ds(pl.multiple_of(start + rows - PAD, SUBS), PAD), :]
+
+    def lanes_of(l):
+        return pl.ds(pl.multiple_of(l * LANES, LANES), LANES)
+
+    sub = lax.broadcasted_iota(jnp.int32, (modes, SUBS, LANES), 1)
+    sub2 = lax.broadcasted_iota(jnp.int32, (SUBS, LANES), 0)
+    wide = (modes, SUBS, LANES)
+
+    def first_pass(block):
+        base = PAD + block * rows
+
+        def tile(l, _):
+            rate = jnp.broadcast_to(decay[:, :, lanes_of(l)], wide)
+            pole = jnp.exp(-rate)
+            taps = [
+                [jnp.broadcast_to(short_w[k, j:j + 1, lanes_of(l)], (SUBS, LANES)) for j in range(3)]
+                for k in range(3)
+            ]
+
+            def at(i):
+                return pl.ds(base + i, SUBS, step_rows)
+
+            def steps(it, carry):
+                s, last, before = carry
+                for u in range(UNROLL):
+                    i = it * UNROLL + u
+                    now = [feat[j * tiles + l, at(i), :] for j in range(3)]
+                    made = [
+                        taps[0][j] * now[j] + taps[1][j] * last[j] + taps[2][j] * before[j]
+                        for j in range(3)
+                    ]
+                    driven = made[1] * made[2]
+                    feat[l, at(i), :] = made[0]
+                    feat[tiles + l, at(i), :] = driven
+                    s = pole * s + driven[None]
+                    last, before = now, last
+                return s, last, before
+
+            there = (sub2 > 0) | (block % 2 == 1)
+
+            def ahead(i):
+                return [
+                    jnp.where(there, feat[j * tiles + l, at(i), :], 0.0) for j in range(3)
+                ]
+
+            s, _, _ = lax.fori_loop(
+                0, step_rows // UNROLL, steps, (jnp.zeros(wide, F32), ahead(-1), ahead(-2))
+            )
+            for shift in (1, 2, 4):
+                fade = jnp.exp(-rate * float(step_rows * shift))
+                s = s + jnp.where(sub >= shift, pltpu.roll(s, shift, 1) * fade, 0.0)
+            excl[block, l] = jnp.where(sub >= 1, pltpu.roll(s, 1, 1), 0.0)
+            block_end[block, l] = s[:, SUBS - 1:SUBS, :]
+            return 0
+
+        lax.fori_loop(0, tiles, tile, 0)
+
+    def first_rows(block):
+        start = pl.ds(pl.multiple_of(PAD + block * rows, SUBS), SUBS)
+
+        def tile(l, _):
+            made = []
+            for j in range(3):
+                own, prior = head[block, j * tiles + l], edge[block, j * tiles + l]
+                last = jnp.where(sub2 < 1, pltpu.roll(prior, 1, 0), pltpu.roll(own, 1, 0))
+                before = jnp.where(sub2 < 2, pltpu.roll(prior, 2, 0), pltpu.roll(own, 2, 0))
+                tap = [
+                    jnp.broadcast_to(short_w[k, j:j + 1, lanes_of(l)], (SUBS, LANES))
+                    for k in range(3)
+                ]
+                made.append(tap[0] * own + tap[1] * last + tap[2] * before)
+            feat[l, start, :] = jnp.where(sub2 < 2, made[0], feat[l, start, :])
+            old = feat[tiles + l, start, :]
+            new = jnp.where(sub2 < 2, made[1] * made[2], old)
+            feat[tiles + l, start, :] = new
+            more = new - old
+            zeroth, first = more[0:1, :][None], more[1:2, :][None]
+            rate = decay[:, :, lanes_of(l)]
+            up = jnp.exp(rate)
+            lag = jnp.maximum(sub * step_rows - 1, 0).astype(F32)
+            fade = jnp.exp(-jnp.broadcast_to(rate, wide) * lag)
+            add = fade * (zeroth + jnp.broadcast_to(up * first, wide))
+            excl[block, l] = excl[block, l] + jnp.where(sub >= 1, add, 0.0)
+            block_end[block, l] = block_end[block, l] + jnp.exp(-rate * float(rows - 1)) * (
+                zeroth + up * first
+            )
+            return 0
+
+        lax.fori_loop(0, tiles, tile, 0)
+
+    for r in range(modes):
+        decay[r] = decay_in[r:r + 1, :]
+        residue[r] = residue_in[r:r + 1, :]
     for load in loads[:4]:
         load.wait()
     project(me)
     arrived(2, cp, whole)
     project(cp)
+    first_pass(me - core + 1)
+    first_pass(me - core)
     arrived(0, xp, top)
     forward(5, xp, top, yp)
     forward(7, xp, top, cp)
@@ -115,6 +211,9 @@
     arrived(8, cp + to_y, low)
     arrived(10, cp + to_y, top)
     project(cp + to_y)
+    for even in (xp - core, yp - core):
+        first_pass(even + 1)
+        first_pass(even)
     arrived(5, diag, top)
     forward(11, diag, top, cp)
     arrived(6, diag, low)
@@ -124,83 +223,30 @@
     arrived(12, diag + to_core, low)
     project(diag + to_core)
 
-    tail = pl.ds(PAD + seq_rows - PAD, PAD)
-    halo_buf[...] = feat[:, tail, :]
     halo = send(
-        halo_buf, feat.at[:, pl.ds(0, PAD)], halo_send, halo_recv, to_ctx=(ctx + 1) % ctxs
+        edge.at[CHAN], edge.at[0], halo_send, halo_recv, to_ctx=(ctx + 1) % ctxs
     )
 
     @pl.when(ctx < ctxs - 1)
     def _():
         halo.start()
 
+    first_pass(diag - core + 1)
+    first_pass(diag - core)
     for copy in sent:
         copy.wait_send()
     for partner in (cp, xp, yp):
         pl.semaphore_signal(credit, inc=1, device_id={"chan": partner}, device_id_type=MESH)
 
-    def lanes_of(l):
-        return pl.ds(pl.multiple_of(l * LANES, LANES), LANES)
-
-    sub = lax.broadcasted_iota(jnp.int32, (modes, SUBS, LANES), 1)
-    wide = (modes, SUBS, LANES)
-
-    def first_pass(block):
-        base = PAD + block * rows
-
-        def tile(l, _):
-            rate = jnp.broadcast_to(decay[:, :, lanes_of(l)], wide)
-            pole = jnp.exp(-rate)
-            taps = [
-                [jnp.broadcast_to(short_w[k, j:j + 1, lanes_of(l)], (SUBS, LANES)) for j in range(3)]
-                for k in range(3)
-            ]
-
-            def at(i):
-                return pl.ds(base + i, SUBS, step_rows)
-
-            def steps(it, carry):
-                s, last, before = carry
-                for u in range(UNROLL):
-                    i = it * UNROLL + u
-                    now = [feat[j * tiles + l, at(i), :] for j in range(3)]
-                    made = [
-                        taps[0][j] * now[j] + taps[1][j] * last[j] + taps[2][j] * before[j]
-                        for j in range(3)
-                    ]
-                    driven = made[1] * made[2]
-                    feat[l, at(i), :] = made[0]
-                    feat[tiles + l, at(i), :] = driven
-                    s = pole * s + driven[None]
-                    last, before = now, last
-                return s, last, before
-
-            s, _, _ = lax.fori_loop(
-                0, step_rows // UNROLL, steps,
-                (
-                    jnp.zeros(wide, F32),
-                    [feat[j * tiles + l, at(-1), :] for j in range(3)],
-                    [feat[j * tiles + l, at(-2), :] for j in range(3)],
-                ),
-            )
-            for shift in (1, 2, 4):
-                fade = jnp.exp(-rate * float(step_rows * shift))
-                s = s + jnp.where(sub >= shift, pltpu.roll(s, shift, 1) * fade, 0.0)
-            excl[block, l] = jnp.where(sub >= 1, pltpu.roll(s, 1, 1), 0.0)
-            block_end[block, l] = s[:, SUBS - 1:SUBS, :]
-            return 0
-
-        lax.fori_loop(0, tiles, tile, 0)
-
-    def backwards(i, _):
-        first_pass(CHAN - 1 - i)
+    def fix(half_block, _):
+        first_rows(2 * half_block)
         return 0
 
-    lax.fori_loop(0, CHAN - 1, backwards, 0)
+    lax.fori_loop(1, CHAN // 2, fix, 0)
 
     @pl.when(ctx == 0)
     def _():
-        feat[:, 0:PAD, :] = jnp.zeros((3 * tiles, PAD, LANES), F32)
+        edge[0] = jnp.zeros((3 * tiles, PAD, LANES), F32)
 
     @pl.when(ctx > 0)
     def _():
@@ -210,7 +256,7 @@
     def _():
         halo.wait_send()
 
-    first_pass(0)
+    first_rows(0)
 
     def own_state(l, _):
         fade = jnp.exp(-decay[:, :, lanes_of(l)] * float(rows))
@@ -286,12 +332,12 @@
 
         lax.fori_loop(0, width // cut, one, 0)
 
-    def multiply(slot, add):
+    def multiply(slot, add, part=whole):
         def body(cols):
-            made = jnp.dot(gated16[...], wo_buf[:, cols], preferred_element_type=F32).astype(BF16)
+            made = jnp.dot(gated16[part, :], wo_buf[:, cols], preferred_element_type=F32).astype(BF16)
             if add:
-                made = (grid_buf[slot, :, cols].astype(F32) + made.astype(F32)).astype(BF16)
-            grid_buf[slot, :, cols] = made
+                made = (grid_buf[slot, part, cols].astype(F32) + made.astype(F32)).astype(BF16)
+            grid_buf[slot, part, cols] = made
 
         over_width(body)
 
@@ -314,21 +360,29 @@
     to_other = []
     for i, mine in enumerate((diag, xp, yp, me)):
         stage = 7 + i % 2
+        parts = ((top, 0), (low, 4)) if i == 0 else ((whole, i),)
         gate(mine + to_core)
         if i >= 2:
-            to_other[i - 2].wait_send()
-        multiply(stage, False)
-        copy = send(
-            grid_buf.at[stage], grid_buf.at[i], cp_send.at[i], cp_recv.at[i], chan=cp
-        )
-        copy.start()
-        to_other.append(copy)
+            for copy in to_other[i - 2]:
+                copy.wait_send()
+        copies = []
+        for part, sem in parts:
+            multiply(stage, False, part)
+            copy = send(
+                grid_buf.at[stage, part], grid_buf.at[i, part],
+                cp_send.at[sem], cp_recv.at[sem], chan=cp,
+            )
+            copy.start()
+            copies.append(copy)
+        to_other.append(copies)
         gate(mine)
-        copy.wait_recv()
-        multiply(i, True)
-        if i == 0:
-            go(0, 0, 4, top, xp)
-            go(1, 0, 4, low, yp)
+        for copy, (part, _) in zip(copies, parts):
+            copy.wait_recv()
+            multiply(i, True, part)
+            if i == 0 and part is top:
+                go(0, 0, 4, top, xp)
+            if i == 0 and part is low:
+                go(1, 0, 4, low, yp)
         if i == 1:
             go(2, 1, 5, top, xp)
         if i == 2:
@@ -349,8 +403,9 @@
     link(0, 0, 4, top, xp).wait_recv()
     join(2, top, 2, 4)
     go(5, 2, 6, top, yp)
-    for copy in to_other[2:]:
-        copy.wait_send()
+    for copies in to_other[2:]:
+        for copy in copies:
+            copy.wait_send()
     results = []
     for h, part, early, late in ((0, top, (2, 5), (5, 6)), (1, low, (3, 6), (4, 5))):
         link(early[0], 0, early[1], part, xp).wait_recv()
@@ -391,9 +446,12 @@
             pltpu.VMEM((ctxs, tiles, modes, 1, LANES), F32),
             pltpu.VMEM((tiles, rows, LANES), F32),
             pltpu.VMEM((rows, chans), BF16),
-            pltpu.VMEM((3 * tiles, PAD, LANES), F32),
+            pltpu.VMEM((CHAN, 3 * tiles, PAD, LANES), F32),
+            pltpu.VMEM((CHAN + 1, 3 * tiles, PAD, LANES), F32),
+            pltpu.VMEM((modes, 1, chans), F32),
+            pltpu.VMEM((modes, 1, chans), F32),
             dma((5,)), dma((13,)), dma((13,)), dma, dma, dma((ctxs,)), dma((ctxs,)),
-            dma((4,)), dma((4,)), dma((6,)), dma((6,)),
+            dma((5,)), dma((5,)), dma((6,)), dma((6,)),
             pltpu.SemaphoreType.REGULAR, dma((2,)),
         ],
         compiler_params=pltpu.CompilerParams(
@@ -406,8 +464,7 @@
         ),
     )(
         tokens, in_weight, short_weight,
-        decay_rate.reshape(modes, 1, chans), residue.reshape(modes, 1, chans),
-        skip_gain.reshape(1, chans), out_weight,
+        decay_rate, residue, skip_gain.reshape(1, chans), out_weight,
     )
 
 

time: 197 us -> 185 us (0.939)
  Pallas kernels: 191 us -> 182 us
  local copies, waits for them, and re-layouts: 5.9 us -> 3.13 us
    pallas_call x1, Pallas kernels: 191 us -> 182 us  [local(): pl.pallas_call(functools.partial(kernel, ctxs), out_shape=jax.ShapeDtypeS...]
    reshape x2 -> x0, local copies, waits for them, and re-layouts: 2.77 us -> none  [the longest x1 1.39 us: local(): decay_rate.reshape(modes, 1, chans)]
where the time goes in v2:
time: 185 us
  Pallas kernels  182 us (98%)
  local copies, waits for them, and re-layouts  3.13 us (2%)
    pallas_call x1, Pallas kernels, local(): pl.pallas_call(functools.partial(kernel, ctxs), out_shape=jax.ShapeDtypeS...  182 us

profile of v2, /device:TPU:0, one launch (start us, length us, event | category | flops | bytes accessed | tf_op | source)
XLA Modules:
  0.0 184.8 jit_solution(2717946978508532311)
XLA Ops:
  0.0 181.6 %shard_map.73 = bf16[256,4096]{1,0:T(8,128)(2,1)} custom-call(bf16[256,4096]{1,0:T(8,128)(2,1)} %tokens.1, bf16[3,4096,512]{2,1,0:T(8,128)(2,1)} %in_w.1, f32[3,3,512]{2,1,0:T(4,128)} %short_w.1, f32[16,512]{1,0:T(8,128)} %decay_in.1, f32[16,512]{1,0:T(8,128)} %residue_in.1, f32[1,512]{1,0:T(1,128)} %bitcast.1, bf16[512,4096]{1,0:T(8,128)(2,1)} %out_w.1), custom_call_target="tpu_custom_call" | custom-call | flops 34359738368 | bytes 20971520 | tf_op jit(solution)/shard_map/pallas_call | solution.py:434
  181.6 3.1 %copy.9 = bf16[256,4096]{1,0:T(8,128)(2,1)} copy(bf16[256,4096]{1,0:T(8,128)(2,1)} %shard_map.73) | data formatting | bytes 4194304

commit v3 on v2

--- a/solution.py
+++ b/solution.py
@@ -17,7 +17,7 @@
 def kernel(
     ctxs, tokens, in_w, short_w, decay_in, residue_in, skip, out_w, out,
     grid_buf, w_buf, wo_buf, feat, excl, block_end, state, gated, gated16,
-    head, edge, decay, residue, load_sem, ag_send, ag_recv, halo_send, halo_recv, st_send, st_recv,
+    query, driven_by, halo_in, decay, residue, load_sem, ag_send, ag_recv, halo_send, halo_recv, st_send, st_recv,
     cp_send, cp_recv, link_send, link_recv, credit, out_sem,
 ):
     ctx, me = lax.axis_index("ctx"), lax.axis_index("chan")
@@ -91,8 +91,6 @@
             return 0
 
         lax.fori_loop(0, 3, kind, 0)
-        head[block] = feat[:, pl.ds(start, PAD), :]
-        edge[block + 1] = feat[:, pl.ds(pl.multiple_of(start + rows - PAD, SUBS), PAD), :]
 
     def lanes_of(l):
         return pl.ds(pl.multiple_of(l * LANES, LANES), LANES)
@@ -100,6 +98,9 @@
     sub = lax.broadcasted_iota(jnp.int32, (modes, SUBS, LANES), 1)
     sub2 = lax.broadcasted_iota(jnp.int32, (SUBS, LANES), 0)
     wide = (modes, SUBS, LANES)
+
+    def stepped(block, i):
+        return pl.ds(pl.multiple_of(block * rows + i * SUBS, SUBS), SUBS)
 
     def first_pass(block):
         base = PAD + block * rows
@@ -125,8 +126,8 @@
                         for j in range(3)
                     ]
                     driven = made[1] * made[2]
-                    feat[l, at(i), :] = made[0]
-                    feat[tiles + l, at(i), :] = driven
+                    query[l, stepped(block, i), :] = made[0]
+                    driven_by[l, stepped(block, i), :] = driven
                     s = pole * s + driven[None]
                     last, before = now, last
                 return s, last, before
@@ -151,12 +152,15 @@
         lax.fori_loop(0, tiles, tile, 0)
 
     def first_rows(block):
-        start = pl.ds(pl.multiple_of(PAD + block * rows, SUBS), SUBS)
+        start = PAD + block * rows
+        at_start = pl.ds(pl.multiple_of(start, SUBS), SUBS)
+        at_prior = pl.ds(pl.multiple_of(start - PAD, SUBS), SUBS)
+        steps = (stepped(block, 0), stepped(block, 1))
 
         def tile(l, _):
             made = []
             for j in range(3):
-                own, prior = head[block, j * tiles + l], edge[block, j * tiles + l]
+                own, prior = feat[j * tiles + l, at_start, :], feat[j * tiles + l, at_prior, :]
                 last = jnp.where(sub2 < 1, pltpu.roll(prior, 1, 0), pltpu.roll(own, 1, 0))
                 before = jnp.where(sub2 < 2, pltpu.roll(prior, 2, 0), pltpu.roll(own, 2, 0))
                 tap = [
@@ -164,12 +168,16 @@
                     for k in range(3)
                 ]
                 made.append(tap[0] * own + tap[1] * last + tap[2] * before)
-            feat[l, start, :] = jnp.where(sub2 < 2, made[0], feat[l, start, :])
-            old = feat[tiles + l, start, :]
-            new = jnp.where(sub2 < 2, made[1] * made[2], old)
-            feat[tiles + l, start, :] = new
-            more = new - old
-            zeroth, first = more[0:1, :][None], more[1:2, :][None]
+            made_driven = made[1] * made[2]
+            more = []
+            for i, at in enumerate(steps):
+                row = jnp.broadcast_to(made[0][i:i + 1, :], (SUBS, LANES))
+                query[l, at, :] = jnp.where(sub2 < 1, row, query[l, at, :])
+                row = jnp.broadcast_to(made_driven[i:i + 1, :], (SUBS, LANES))
+                old = driven_by[l, at, :]
+                driven_by[l, at, :] = jnp.where(sub2 < 1, row, old)
+                more.append((row - old)[0:1, :][None])
+            zeroth, first = more
             rate = decay[:, :, lanes_of(l)]
             up = jnp.exp(rate)
             lag = jnp.maximum(sub * step_rows - 1, 0).astype(F32)
@@ -224,7 +232,8 @@
     project(diag + to_core)
 
     halo = send(
-        edge.at[CHAN], edge.at[0], halo_send, halo_recv, to_ctx=(ctx + 1) % ctxs
+        feat.at[:, pl.ds(seq_rows, PAD)], halo_in, halo_send, halo_recv,
+        to_ctx=(ctx + 1) % ctxs,
     )
 
     @pl.when(ctx < ctxs - 1)
@@ -246,11 +255,12 @@
 
     @pl.when(ctx == 0)
     def _():
-        edge[0] = jnp.zeros((3 * tiles, PAD, LANES), F32)
+        feat[:, 0:PAD, :] = jnp.zeros((3 * tiles, PAD, LANES), F32)
 
     @pl.when(ctx > 0)
     def _():
         halo.wait_recv()
+        feat[:, 0:PAD, :] = halo_in[...]
 
     @pl.when(ctx < ctxs - 1)
     def _():
@@ -298,8 +308,6 @@
     lax.fori_loop(0, tiles, enter, 0)
 
     def gate(block):
-        base = PAD + block * rows
-
         def tile(l, _):
             rate = jnp.broadcast_to(decay[:, :, lanes_of(l)], wide)
             pole = jnp.exp(-rate)
@@ -309,11 +317,12 @@
             def steps(it, s):
                 for u in range(UNROLL):
                     i = it * UNROLL + u
-                    at = pl.ds(base + i, SUBS, step_rows)
-                    driven = feat[tiles + l, at, :]
+                    driven = driven_by[l, stepped(block, i), :]
                     s = pole * s + driven[None]
                     y = jnp.sum(gain * s, axis=0) + direct * driven
-                    gated[l, pl.ds(i, SUBS, step_rows), :] = feat[l, at, :] * y
+                    gated[l, pl.ds(i, SUBS, step_rows), :] = (
+                        query[l, stepped(block, i), :] * y
+                    )
                 return s
 
             lax.fori_loop(0, step_rows // UNROLL, steps, excl[block, l])
@@ -446,8 +455,9 @@
             pltpu.VMEM((ctxs, tiles, modes, 1, LANES), F32),
             pltpu.VMEM((tiles, rows, LANES), F32),
             pltpu.VMEM((rows, chans), BF16),
-            pltpu.VMEM((CHAN, 3 * tiles, PAD, LANES), F32),
-            pltpu.VMEM((CHAN + 1, 3 * tiles, PAD, LANES), F32),
+            pltpu.VMEM((tiles, seq_rows, LANES), F32),
+            pltpu.VMEM((tiles, seq_rows, LANES), F32),
+            pltpu.VMEM((3 * tiles, PAD, LANES), F32),
             pltpu.VMEM((modes, 1, chans), F32),
             pltpu.VMEM((modes, 1, chans), F32),
             dma((5,)), dma((13,)), dma((13,)), dma, dma, dma((ctxs,)), dma((ctxs,)),

time: 185 us -> 182 us (0.984)
  Pallas kernels: 182 us -> 179 us
    pallas_call x1, Pallas kernels: 182 us -> 179 us  [local(): pl.pallas_call(functools.partial(kernel, ctxs), out_shape=jax.ShapeDtypeS...]
where the time goes in v3:
time: 182 us
  Pallas kernels  179 us (98%)
  local copies, waits for them, and re-layouts  3.13 us (2%)
    pallas_call x1, Pallas kernels, local(): pl.pallas_call(functools.partial(kernel, ctxs), out_shape=jax.ShapeDtypeS...  179 us

profile of v3, /device:TPU:0, one launch (start us, length us, event | category | flops | bytes accessed | tf_op | source)
XLA Modules:
  0.0 181.7 jit_solution(14313674009117587367)
XLA Ops:
  0.0 178.6 %shard_map.73 = bf16[256,4096]{1,0:T(8,128)(2,1)} custom-call(bf16[256,4096]{1,0:T(8,128)(2,1)} %tokens.1, bf16[3,4096,512]{2,1,0:T(8,128)(2,1)} %in_w.1, f32[3,3,512]{2,1,0:T(4,128)} %short_w.1, f32[16,512]{1,0:T(8,128)} %decay_in.1, f32[16,512]{1,0:T(8,128)} %residue_in.1, f32[1,512]{1,0:T(1,128)} %bitcast.1, bf16[512,4096]{1,0:T(8,128)(2,1)} %out_w.1), custom_call_target="tpu_custom_call" | custom-call | flops 34359738368 | bytes 20971520 | tf_op jit(solution)/shard_map/pallas_call | solution.py:443
  178.6 3.1 %copy.9 = bf16[256,4096]{1,0:T(8,128)(2,1)} copy(bf16[256,4096]{1,0:T(8,128)(2,1)} %shard_map.73) | data formatting | bytes 4194304

commit v4 on v3

--- a/solution.py
+++ b/solution.py
@@ -17,7 +17,7 @@
 def kernel(
     ctxs, tokens, in_w, short_w, decay_in, residue_in, skip, out_w, out,
     grid_buf, w_buf, wo_buf, feat, excl, block_end, state, gated, gated16,
-    query, driven_by, halo_in, decay, residue, load_sem, ag_send, ag_recv, halo_send, halo_recv, st_send, st_recv,
+    driven_by, halo_in, decay, residue, load_sem, ag_send, ag_recv, halo_send, halo_recv, st_send, st_recv,
     cp_send, cp_recv, link_send, link_recv, credit, out_sem,
 ):
     ctx, me = lax.axis_index("ctx"), lax.axis_index("chan")
@@ -80,7 +80,7 @@
     def arrived(i, block, part):
         hop(i, block, part, cp).wait_recv()
 
-    def project(block):
+    def project(block, first=0, last=3):
         start = pl.multiple_of(PAD + block * rows, SUBS)
 
         def kind(j, _):
@@ -90,7 +90,7 @@
                 feat[j * tiles + l, pl.ds(start, rows), :] = made[:, l * LANES:(l + 1) * LANES]
             return 0
 
-        lax.fori_loop(0, 3, kind, 0)
+        lax.fori_loop(first, last, kind, 0)
 
     def lanes_of(l):
         return pl.ds(pl.multiple_of(l * LANES, LANES), LANES)
@@ -109,7 +109,7 @@
             rate = jnp.broadcast_to(decay[:, :, lanes_of(l)], wide)
             pole = jnp.exp(-rate)
             taps = [
-                [jnp.broadcast_to(short_w[k, j:j + 1, lanes_of(l)], (SUBS, LANES)) for j in range(3)]
+                [jnp.broadcast_to(short_w[k, j:j + 1, lanes_of(l)], (SUBS, LANES)) for j in (1, 2)]
                 for k in range(3)
             ]
 
@@ -120,13 +120,12 @@
                 s, last, before = carry
                 for u in range(UNROLL):
                     i = it * UNROLL + u
-                    now = [feat[j * tiles + l, at(i), :] for j in range(3)]
+                    now = [feat[j * tiles + l, at(i), :] for j in (1, 2)]
                     made = [
                         taps[0][j] * now[j] + taps[1][j] * last[j] + taps[2][j] * before[j]
-                        for j in range(3)
+                        for j in range(2)
                     ]
-                    driven = made[1] * made[2]
-                    query[l, stepped(block, i), :] = made[0]
+                    driven = made[0] * made[1]
                     driven_by[l, stepped(block, i), :] = driven
                     s = pole * s + driven[None]
                     last, before = now, last
@@ -136,7 +135,7 @@
 
             def ahead(i):
                 return [
-                    jnp.where(there, feat[j * tiles + l, at(i), :], 0.0) for j in range(3)
+                    jnp.where(there, feat[j * tiles + l, at(i), :], 0.0) for j in (1, 2)
                 ]
 
             s, _, _ = lax.fori_loop(
@@ -159,7 +158,7 @@
 
         def tile(l, _):
             made = []
-            for j in range(3):
+            for j in (1, 2):
                 own, prior = feat[j * tiles + l, at_start, :], feat[j * tiles + l, at_prior, :]
                 last = jnp.where(sub2 < 1, pltpu.roll(prior, 1, 0), pltpu.roll(own, 1, 0))
                 before = jnp.where(sub2 < 2, pltpu.roll(prior, 2, 0), pltpu.roll(own, 2, 0))
@@ -168,11 +167,9 @@
                     for k in range(3)
                 ]
                 made.append(tap[0] * own + tap[1] * last + tap[2] * before)
-            made_driven = made[1] * made[2]
+            made_driven = made[0] * made[1]
             more = []
             for i, at in enumerate(steps):
-                row = jnp.broadcast_to(made[0][i:i + 1, :], (SUBS, LANES))
-                query[l, at, :] = jnp.where(sub2 < 1, row, query[l, at, :])
                 row = jnp.broadcast_to(made_driven[i:i + 1, :], (SUBS, LANES))
                 old = driven_by[l, at, :]
                 driven_by[l, at, :] = jnp.where(sub2 < 1, row, old)
@@ -226,15 +223,19 @@
     forward(11, diag, top, cp)
     arrived(6, diag, low)
     forward(12, diag, low, cp)
-    project(diag)
+    project(diag, 1)
     arrived(11, diag + to_core, top)
     arrived(12, diag + to_core, low)
-    project(diag + to_core)
-
-    halo = send(
-        feat.at[:, pl.ds(seq_rows, PAD)], halo_in, halo_send, halo_recv,
-        to_ctx=(ctx + 1) % ctxs,
-    )
+    project(diag + to_core, 1)
+
+    def halo_of(i, kinds):
+        return send(
+            feat.at[kinds, pl.ds(seq_rows, PAD)], halo_in.at[kinds],
+            halo_send.at[i], halo_recv.at[i], to_ctx=(ctx + 1) % ctxs,
+        )
+
+    queries, drives = pl.ds(0, tiles), pl.ds(tiles, 2 * tiles)
+    halo, query_halo = halo_of(0, drives), halo_of(1, queries)
 
     @pl.when(ctx < ctxs - 1)
     def _():
@@ -244,8 +245,6 @@
     first_pass(diag - core)
     for copy in sent:
         copy.wait_send()
-    for partner in (cp, xp, yp):
-        pl.semaphore_signal(credit, inc=1, device_id={"chan": partner}, device_id_type=MESH)
 
     def fix(half_block, _):
         first_rows(2 * half_block)
@@ -260,7 +259,7 @@
     @pl.when(ctx > 0)
     def _():
         halo.wait_recv()
-        feat[:, 0:PAD, :] = halo_in[...]
+        feat[drives, 0:PAD, :] = halo_in[drives]
 
     @pl.when(ctx < ctxs - 1)
     def _():
@@ -285,6 +284,16 @@
         )
         copy.start()
         state_copies.append(copy)
+
+    project(diag, 0, 1)
+    project(diag + to_core, 0, 1)
+    for partner in (cp, xp, yp):
+        pl.semaphore_signal(credit, inc=1, device_id={"chan": partner}, device_id_type=MESH)
+
+    @pl.when(ctx < ctxs - 1)
+    def _():
+        query_halo.start()
+
     for off in range(1, ctxs):
         source = (ctx + ctxs - off) % ctxs
         send(
@@ -307,6 +316,15 @@
 
     lax.fori_loop(0, tiles, enter, 0)
 
+    @pl.when(ctx > 0)
+    def _():
+        query_halo.wait_recv()
+        feat[queries, 0:PAD, :] = halo_in[queries]
+
+    @pl.when(ctx < ctxs - 1)
+    def _():
+        query_halo.wait_send()
+
     def gate(block):
         def tile(l, _):
             rate = jnp.broadcast_to(decay[:, :, lanes_of(l)], wide)
@@ -320,12 +338,15 @@
                     driven = driven_by[l, stepped(block, i), :]
                     s = pole * s + driven[None]
                     y = jnp.sum(gain * s, axis=0) + direct * driven
-                    gated[l, pl.ds(i, SUBS, step_rows), :] = (
-                        query[l, stepped(block, i), :] * y
-                    )
+                    gated[l, pl.ds(i, SUBS, step_rows), :] = y
                 return s
 
             lax.fori_loop(0, step_rows // UNROLL, steps, excl[block, l])
+            query = sum(
+                short_w[k, 0:1, lanes_of(l)] * feat[l, pl.ds(PAD + block * rows - k, rows), :]
+                for k in range(3)
+            )
+            gated[l] = query * gated[l]
             return 0
 
         lax.fori_loop(0, tiles, tile, 0)
@@ -456,11 +477,10 @@
             pltpu.VMEM((tiles, rows, LANES), F32),
             pltpu.VMEM((rows, chans), BF16),
             pltpu.VMEM((tiles, seq_rows, LANES), F32),
-            pltpu.VMEM((tiles, seq_rows, LANES), F32),
             pltpu.VMEM((3 * tiles, PAD, LANES), F32),
             pltpu.VMEM((modes, 1, chans), F32),
             pltpu.VMEM((modes, 1, chans), F32),
-            dma((5,)), dma((13,)), dma((13,)), dma, dma, dma((ctxs,)), dma((ctxs,)),
+            dma((5,)), dma((13,)), dma((13,)), dma((2,)), dma((2,)), dma((ctxs,)), dma((ctxs,)),
             dma((5,)), dma((5,)), dma((6,)), dma((6,)),
             pltpu.SemaphoreType.REGULAR, dma((2,)),
         ],

time: 182 us -> 177 us (0.973)
  Pallas kernels: 179 us -> 174 us
    pallas_call x1, Pallas kernels: 179 us -> 174 us  [local(): pl.pallas_call(functools.partial(kernel, ctxs), out_shape=jax.ShapeDtypeS...]
where the time goes in v4:
time: 177 us
  Pallas kernels  174 us (98%)
  local copies, waits for them, and re-layouts  3.13 us (2%)
    pallas_call x1, Pallas kernels, local(): pl.pallas_call(functools.partial(kernel, ctxs), out_shape=jax.ShapeDtypeS...  174 us

profile of v4, /device:TPU:0, one launch (start us, length us, event | category | flops | bytes accessed | tf_op | source)
XLA Modules:
  0.0 177.1 jit_solution(9023744642344435352)
XLA Ops:
  0.0 173.9 %shard_map.73 = bf16[256,4096]{1,0:T(8,128)(2,1)} custom-call(bf16[256,4096]{1,0:T(8,128)(2,1)} %tokens.1, bf16[3,4096,512]{2,1,0:T(8,128)(2,1)} %in_w.1, f32[3,3,512]{2,1,0:T(4,128)} %short_w.1, f32[16,512]{1,0:T(8,128)} %decay_in.1, f32[16,512]{1,0:T(8,128)} %residue_in.1, f32[1,512]{1,0:T(1,128)} %bitcast.1, bf16[512,4096]{1,0:T(8,128)(2,1)} %out_w.1), custom_call_target="tpu_custom_call" | custom-call | flops 34359738368 | bytes 20971520 | tf_op jit(solution)/shard_map/pallas_call | solution.py:464
  173.9 3.1 %copy.9 = bf16[256,4096]{1,0:T(8,128)(2,1)} copy(bf16[256,4096]{1,0:T(8,128)(2,1)} %shard_map.73) | data formatting | bytes 4194304

commit v5 on v4

--- a/solution.py
+++ b/solution.py
@@ -216,14 +216,15 @@
     arrived(8, cp + to_y, low)
     arrived(10, cp + to_y, top)
     project(cp + to_y)
-    for even in (xp - core, yp - core):
-        first_pass(even + 1)
-        first_pass(even)
+    first_pass(xp - core + 1)
+    first_pass(xp - core)
+    first_pass(yp - core + 1)
     arrived(5, diag, top)
     forward(11, diag, top, cp)
     arrived(6, diag, low)
     forward(12, diag, low, cp)
     project(diag, 1)
+    first_pass(yp - core)
     arrived(11, diag + to_core, top)
     arrived(12, diag + to_core, low)
     project(diag + to_core, 1)

time: 177 us -> 176 us (level)
  no operation moved by 1% of the time
where the time goes in v5:
time: 176 us
  Pallas kernels  173 us (98%)
  local copies, waits for them, and re-layouts  3.13 us (2%)
    pallas_call x1, Pallas kernels, local(): pl.pallas_call(functools.partial(kernel, ctxs), out_shape=jax.ShapeDtypeS...  173 us

profile of v5, /device:TPU:0, one launch (start us, length us, event | category | flops | bytes accessed | tf_op | source)
XLA Modules:
  0.0 176.1 jit_solution(1342638667439955643)
XLA Ops:
  0.0 173.0 %shard_map.73 = bf16[256,4096]{1,0:T(8,128)(2,1)} custom-call(bf16[256,4096]{1,0:T(8,128)(2,1)} %tokens.1, bf16[3,4096,512]{2,1,0:T(8,128)(2,1)} %in_w.1, f32[3,3,512]{2,1,0:T(4,128)} %short_w.1, f32[16,512]{1,0:T(8,128)} %decay_in.1, f32[16,512]{1,0:T(8,128)} %residue_in.1, f32[1,512]{1,0:T(1,128)} %bitcast.1, bf16[512,4096]{1,0:T(8,128)(2,1)} %out_w.1), custom_call_target="tpu_custom_call" | custom-call | flops 34359738368 | bytes 20971520 | tf_op jit(solution)/shard_map/pallas_call | solution.py:465
  173.0 3.1 %copy.9 = bf16[256,4096]{1,0:T(8,128)(2,1)} copy(bf16[256,4096]{1,0:T(8,128)(2,1)} %shard_map.73) | data formatting | bytes 4194304
